TPU v7x, 32 devices: a whole 2x2x4 slice. The times are simulated.
32 devices in a mesh: groups: 2 (over y), gx: 4 (over z), gy: 4 (over x, core).
Axes of the slice: x: 2, y: 2, z: 4, core: 2. Of those that a mesh axis runs over, the one named last changes fastest.
Arguments:
- tokens: bfloat16 [128, 8192], P(('groups', 'gx'), 'gy'), parts along dimension 0, may hold values from -220 to 220
- norm_gain: float32 [8192], P('gy'), may hold values from 0.85 to 12
- w_query: bfloat16 [8192, 8192], P('gy', 'gx'), may hold values from -0.0625 to 0.0625
- keyvalue_weight: bfloat16 [8192, 2048], P('gy', 'gx'), may hold values from -0.0625 to 0.0625
- w_out: bfloat16 [8192, 8192], P('gy', 'gx'), may hold values from -0.0625 to 0.0625
- segment_ids: int32 [8, 16], P(('groups', 'gx')), parts along dimension 0, may hold values from 0 to 2, never falling along the last dimension, each value on 1 to 8 neighbouring positions
Outputs:
- attn_out: bfloat16 [128, 8192], P(('groups', 'gy'), 'gx'), parts along dimension 0
There are 2 independent parts, one for each index of `groups`. A program takes and returns all parts, laid end to end along the dimension named above; an argument that names none is the same for every part. Nothing has to cross between parts.
Inputs may be any that keep to these rules, and one draw needn't show every extreme that they name: `segment_ids`: in each request the ids never fall along the rows; every id of 0 to 2 covers 1 to 8 consecutive rows, some id exactly 8.
All inputs are finite; a program needn't handle non-finite values.
Results may differ from a plain program's by a relative error of at most 0.00405.
The roundings to bfloat16 on the way count: a program that leaves them out, or rounds other values in their place, can miss the bound.
Values may be sent and summed in bfloat16 or wider, within the bound.
A program may use at most 64 MiB of HBM per device.

v0:
```python
import jax
import jax.numpy as jnp
from jax import lax
from jax.sharding import PartitionSpec as P

MODEL_WIDTH = 8192
QUERY_HEADS = 64
KEYVALUE_HEADS = 8
HEAD_WIDTH = 128
SEGS = 3


EPSILON = 1e-05
ROPE_BASE = 500000.0
MASK_VALUE = -1e30


def row_positions(segments, segment_total):
    bounds = jnp.arange(segment_total + 1, dtype=jnp.int32)
    first_rows = jnp.sum((segments[:, None, :] < bounds[None, :, None]).astype(jnp.int32), axis=2)
    matches = segments[:, :, None] == bounds[None, None, :segment_total]
    segment_first = jnp.sum(jnp.where(matches, first_rows[:, None, :segment_total], 0), axis=2)
    context_length = first_rows[:, 1:2]
    row_index = jnp.arange(segments.shape[1], dtype=jnp.int32)[None, :]
    positions = jnp.where(segments == 0, row_index, context_length + row_index - segment_first)
    return positions.reshape(-1)


def rotate(values, positions):
    half_size = values.shape[-1] // 2
    frequency = ROPE_BASE ** (-2.0 * jnp.arange(half_size, dtype=jnp.float32) / values.shape[-1])
    angle = positions.astype(jnp.float32)[:, None, None] * frequency[None, None, :]
    cosine = jnp.cos(angle)
    sine = jnp.sin(angle)
    first_half = values[..., :half_size]
    second_half = values[..., half_size:]
    return jnp.concatenate(
        [first_half * cosine - second_half * sine, second_half * cosine + first_half * sine],
        axis=-1,
    )


def request_mask(segments):
    row_index = jnp.arange(segments.shape[0], dtype=jnp.int32)
    causal = row_index[None, :] <= row_index[:, None]
    same_part = (segments[None, :] == segments[:, None]) | (segments[None, :] == 0)
    return causal & same_part


def on_device(tokens, norm_gain, w_query, keyvalue_weight, w_out, segment_ids):
    column_group_count = lax.axis_size("gy")
    gy_index = lax.axis_index("gy")
    rows_here = tokens.shape[0]
    query_cols = w_query.shape[1]
    head_block = QUERY_HEADS // column_group_count
    keyvalue_block = KEYVALUE_HEADS // column_group_count
    group_width = QUERY_HEADS // KEYVALUE_HEADS
    query_width = head_block * HEAD_WIDTH
    keyval_width = keyvalue_block * 2 * HEAD_WIDTH
    local_positions = row_positions(segment_ids, SEGS)
    widened = tokens.astype(jnp.float32)
    squares = lax.psum(jnp.sum(widened * widened, axis=1), "gy")
    widened = tokens.astype(jnp.float32)
    normalized_input = (
        widened * lax.rsqrt(squares / MODEL_WIDTH + EPSILON)[:, None] * norm_gain[None, :]
    ).astype(jnp.bfloat16)
    piece_rows = lax.all_gather(normalized_input, "gx", axis=0, tiled=True)
    partial_heads = jnp.concatenate(
        [
            jnp.dot(piece_rows, w_query, preferred_element_type=jnp.float32),
            jnp.dot(piece_rows, keyvalue_weight, preferred_element_type=jnp.float32),
        ],
        axis=1,
    )
    query_part = partial_heads[:, :query_cols]
    keyval_part = partial_heads[:, query_cols:]
    query_sum, keyval_sum = lax.psum((query_part, keyval_part), "gy")
    query_rows, keyval_rows = (
        lax.all_to_all(query_sum, "gx", split_axis=0, concat_axis=1, tiled=True),
        lax.all_to_all(keyval_sum, "gx", split_axis=0, concat_axis=1, tiled=True),
    )
    query_here = lax.dynamic_slice_in_dim(query_rows, gy_index * query_width, query_width, 1)
    keyval_here = lax.dynamic_slice_in_dim(keyval_rows, gy_index * keyval_width, keyval_width, 1)
    heads_of_query = rotate(
        query_here.reshape(rows_here, head_block, HEAD_WIDTH), local_positions
    ).astype(jnp.bfloat16)
    heads_of_query = heads_of_query.reshape(rows_here, keyvalue_block, group_width, HEAD_WIDTH)
    keyvalue_pairs = keyval_here.reshape(rows_here, keyvalue_block, 2, HEAD_WIDTH)
    key_heads = rotate(keyvalue_pairs[:, :, 0], local_positions).astype(jnp.bfloat16)
    value_heads = keyvalue_pairs[:, :, 1].astype(jnp.bfloat16)
    score_scale = HEAD_WIDTH ** (-0.5)
    scores = (
        jnp.einsum("rkgd,tkd->kgrt", heads_of_query, key_heads, preferred_element_type=jnp.float32)
        * score_scale
    )
    visible = request_mask(segment_ids[0])
    scores = jnp.where(visible[None, None], scores, MASK_VALUE)
    row_top = jnp.max(scores, axis=-1, keepdims=True)
    weights = jnp.exp(scores - row_top)
    probabilities = (weights / jnp.sum(weights, axis=-1, keepdims=True)).astype(jnp.bfloat16)
    mixed_heads = jnp.einsum(
        "kgrt,tkd->rkgd", probabilities, value_heads, preferred_element_type=jnp.float32
    )
    mixed = mixed_heads.astype(jnp.bfloat16).reshape(rows_here, query_width)
    output_terms = jnp.dot(
        lax.all_gather(mixed, "gx", axis=0, tiled=True), w_out, preferred_element_type=jnp.float32
    )
    return lax.psum_scatter(output_terms, "gy", scatter_dimension=0, tiled=True).astype(
        jnp.bfloat16
    )


def solution(mesh):
    return jax.shard_map(
        on_device,
        mesh=mesh,
        in_specs=(
            P(("groups", "gx"), "gy"),
            P("gy"),
            P("gy", "gx"),
            P("gy", "gx"),
            P("gy", "gx"),
            P(("groups", "gx"), None),
        ),
        out_specs=P(("groups", "gy"), "gx"),
        check_vma=False,
    )
```

profile of v0, /device:TPU:0, one launch (start us, length us, event | category | flops | bytes accessed | tf_op | source)
XLA Modules:
  0.0 149.2 jit_solution(1009213313060652359)
XLA Ops:
  6.5 0.0 copy-start
  6.5 0.0 all-reduce.3.cloned.1.call-start
  6.5 1.1 fusion.6
  7.7 8.3 %psum.21 = f32[16]{0:T(128)S(1)} all-reduce(f32[16]{0:T(128)S(1)} %fusion.6), channel_id=1, replica_groups=mesh['groups'=2,'gx'=4,'gy'=4] {'gy'}, use_global_device_ids=true, to_apply=%region_1.2 | all-reduce | flops 16 | bytes 128 | tf_op jit(solution)/shard_map/psum | solution.py:62
  16.0 0.9 fusion.8
  16.9 14.1 %all_gather.6 = bf16[64,2048]{1,0:T(8,128)(2,1)S(1)} all-gather(bf16[16,2048]{1,0:T(8,128)(2,1)S(1)} %fusion.8), channel_id=1, replica_groups=mesh['groups'=2,'gx'=4,'gy'=4] {'gx'}, dimensions={0}, use_global_device_ids=true | all-gather | bytes 327680 | tf_op jit(solution)/shard_map/all_gather | solution.py:67
  31.1 5.8 %fusion.44 = f32[64,2048]{1,0:T(8,128)} fusion(bf16[64,2048]{1,0:T(8,128)(2,1)S(1)} %all_gather.6, bf16[2048,2048]{1,0:T(8,128)(2,1)} %param.8), kind=kOutput, calls=%fused_computation.55 | convolution fusion | flops 536870912 | bytes 9175040 | tf_op jit(solution)/shard_map/dot_general | solution.py:70
  36.8 0.0 copy-done
  36.9 1.1 fusion.43
  38.0 0.0 all-reduce.3.cloned.1.call-update
  38.0 0.0 copy-done.1
  38.0 0.1 convert_reduce_fusion
  38.1 0.6 slice.31
  38.7 0.1 fusion.21
  38.8 33.8 %all-reduce.3.cloned.1.call-done = (f32[4,16,2048]{2,1,0:T(8,128)}, f32[4,16,512]{2,1,0:T(8,128)}) async-done(((f32[4,16,2048]{2,1,0:T(8,128)}, f32[4,16,512]{2,1,0:T(8,128)}), (f32[4,16,2048]{2,1,0:T(8,128)}, f32[4,16,512]{2,1,0:T(8,128)})) %all-reduce.3.cloned.1.call-update) | async-done | bytes 655376 | tf_op jit(solution)/shard_map/psum | solution.py:77
  72.7 4.6 %all-to-all-start = ((f32[4,16,512]{2,1,0:T(8,128)}), f32[4,16,512]{2,1,0:T(8,128)S(1)}, u32[]{:S(2)}, u32[]{:S(2)}) async-start(f32[4,16,512]{2,1,0:T(8,128)} %get-tuple-element.6), calls=%async_computation | async-start | bytes 262144 | tf_op jit(solution)/shard_map/all_to_all | solution.py:80
  77.3 0.1 fusion.20
  77.3 5.8 %all-to-all-done = f32[4,16,512]{2,1,0:T(8,128)S(1)} async-done(((f32[4,16,512]{2,1,0:T(8,128)}), f32[4,16,512]{2,1,0:T(8,128)S(1)}, u32[]{:S(2)}, u32[]{:S(2)}) %all-to-all-start) | async-done | bytes 131104 | tf_op jit(solution)/shard_map/all_to_all | solution.py:80
  83.2 3.5 %all-to-all-start.1 = ((f32[4,16,2048]{2,1,0:T(8,128)}), f32[4,16,2048]{2,1,0:T(8,128)S(1)}, u32[]{:S(2)}, u32[]{:S(2)}) async-start(f32[4,16,2048]{2,1,0:T(8,128)} %get-tuple-element.5), calls=%async_computation.1 | async-start | bytes 1048576 | tf_op jit(solution)/shard_map/all_to_all | solution.py:79
  86.7 0.0 reduce-scatter.2.cloned.1.call-start
  86.7 0.7 fusion.23
  87.4 0.1 multiply_cosine_fusion
  87.6 0.1 subtract_convert_fusion.1
  87.7 11.3 %all-to-all-done.1 = f32[4,16,2048]{2,1,0:T(8,128)S(1)} async-done(((f32[4,16,2048]{2,1,0:T(8,128)}), f32[4,16,2048]{2,1,0:T(8,128)S(1)}, u32[]{:S(2)}, u32[]{:S(2)}) %all-to-all-start.1) | async-done | bytes 524320 | tf_op jit(solution)/shard_map/all_to_all | solution.py:79
  99.1 0.1 subtract_convert_fusion
  99.3 0.4 fusion.40
  99.7 0.5 fusion.5
  100.3 14.4 %all_gather.7 = bf16[64,2048]{1,0:T(8,128)(2,1)S(1)} all-gather(bf16[16,2048]{1,0:T(8,128)(2,1)S(1)} %bitcast.81), channel_id=1, replica_groups=mesh['groups'=2,'gx'=4,'gy'=4] {'gx'}, dimensions={0}, use_global_device_ids=true | all-gather | bytes 327680 | tf_op jit(solution)/shard_map/all_gather | solution.py:106
  114.7 5.7 %fusion.45 = f32[64,2048]{1,0:T(8,128)} fusion(bf16[64,2048]{1,0:T(8,128)(2,1)S(1)} %all_gather.7, bf16[2048,2048]{1,0:T(8,128)(2,1)} %param.10), kind=kOutput, calls=%fused_computation.56 | convolution fusion | flops 536870912 | bytes 9175040 | tf_op jit(solution)/shard_map/dot_general | solution.py:105
  120.4 0.0 reduce-scatter.2.cloned.1.call-update
  120.4 20.4 %reduce-scatter.2.cloned.1.call-done = f32[16,2048]{1,0:T(8,128)} async-done(((f32[64,2048]{1,0:T(8,128)}), f32[16,2048]{1,0:T(8,128)}) %reduce-scatter.2.cloned.1.call-update) | async-done | bytes 131088 | tf_op jit(solution)/shard_map/reduce_scatter | solution.py:108
  140.9 1.5 %convert_element_type.57 = bf16[16,2048]{1,0:T(8,128)(2,1)} convert(f32[16,2048]{1,0:T(8,128)} %reduce-scatter.2.cloned.1.call-done) | non-fusion elementwise | flops 32768 | bytes 196608 | tf_op jit(solution)/shard_map/convert_element_type | solution.py:108
  (19 shorter events, 0.3 us)
Async XLA Ops:
  6.5 30.3 %copy-start = (bf16[2048,512]{1,0:T(8,128)(2,1)S(1)}, bf16[2048,512]{1,0:T(8,128)(2,1)}, u32[]{:S(2)}) copy-start(bf16[2048,512]{1,0:T(8,128)(2,1)} %param.9) | copy-start | bytes 6291460
  6.5 66.1 %all-reduce.3.cloned.1.call-start = ((), (), s32[]{:S(2)}) async-start(), calls=%async_computation.4 | async-start | bytes 1310720 | tf_op jit(solution)/shard_map/psum | solution.py:77
  31.1 6.9 %copy-start.1 = (s32[1,16]{1,0:T(1,128)S(1)}, s32[1,16]{1,0:T(1,128)}, u32[]{:S(2)}) copy-start(s32[1,16]{1,0:T(1,128)} %param.11) | copy-start | bytes 196
  72.7 10.5 %all-to-all-start = ((f32[4,16,512]{2,1,0:T(8,128)}), f32[4,16,512]{2,1,0:T(8,128)S(1)}, u32[]{:S(2)}, u32[]{:S(2)}) async-start(f32[4,16,512]{2,1,0:T(8,128)} %get-tuple-element.6), calls=%async_computation | async-start | bytes 262144 | tf_op jit(solution)/shard_map/all_to_all | solution.py:80
  83.2 15.8 %all-to-all-start.1 = ((f32[4,16,2048]{2,1,0:T(8,128)}), f32[4,16,2048]{2,1,0:T(8,128)S(1)}, u32[]{:S(2)}, u32[]{:S(2)}) async-start(f32[4,16,2048]{2,1,0:T(8,128)} %get-tuple-element.5), calls=%async_computation.1 | async-start | bytes 1048576 | tf_op jit(solution)/shard_map/all_to_all | solution.py:79
  86.7 54.2 %reduce-scatter.2.cloned.1.call-start = ((), (), s32[]{:S(2)}) async-start(), calls=%async_computation.3 | async-start | bytes 655360 | tf_op jit(solution)/shard_map/reduce_scatter | solution.py:108
Sparse Core Ops, SparseCore 0:
  38.1 34.4 all-reduce.2
  120.5 20.2 reduce-scatter.1
where the time goes:
time: 150 us; the launch traced here: 149 us
  waiting for transfers between devices  71.4 us (48%)
  blocking collectives  36.8 us (25%)
  matrix products  13.6 us (9%)
  between operations  13.6 us (9%)
  starting transfers between devices  8.11 us (5%)
  other arithmetic  4.85 us (3%)
    psum x1, waiting for transfers between devices, on_device(): query_sum, keyval_sum = lax.psum((query_part, keyval_part), 'gy')  33.8 us
    reduce_scatter x1, waiting for transfers between devices, on_device(): lax.psum_scatter(output_terms, 'gy', scatter_dimension=0, tiled=True)  20.4 us
    all_gather x1, blocking collectives, on_device(): lax.all_gather(mixed, 'gx', axis=0, tiled=True)  14.4 us
    all_gather x1, blocking collectives, on_device(): piece_rows = lax.all_gather(normalized_input, 'gx', axis=0, tiled=True)  14.1 us
    all_to_all x1, waiting for transfers between devices, on_device(): lax.all_to_all(query_sum, 'gx', split_axis=0, concat_axis=1, tiled=True)  11.3 us
    psum x1, blocking collectives, on_device(): squares = lax.psum(jnp.sum(widened * widened, axis=1), 'gy')  8.34 us
    all_to_all x1, waiting for transfers between devices, on_device(): lax.all_to_all(keyval_sum, 'gx', split_axis=0, concat_axis=1, tiled=True)  5.84 us
    dot_general x1, matrix products, on_device(): jnp.dot(piece_rows, w_query, preferred_element_type=jnp.float32)  5.78 us
  transfers between devices with their start and end apart: 4, of which 4 were waited for; matrix products, arithmetic and copies ran while one was open for 1% of the time, Pallas kernels for 0%

commit v1 on v0

--- a/solution.py
+++ b/solution.py
@@ -1,6 +1,10 @@
+import functools
+
 import jax
 import jax.numpy as jnp
 from jax import lax
+from jax.experimental import pallas as pl
+from jax.experimental.pallas import tpu as pltpu
 from jax.sharding import PartitionSpec as P
 
 MODEL_WIDTH = 8192
@@ -110,9 +114,345 @@
     )
 
 
+MESH = pl.DeviceIdType.MESH
+TILE = 512
+
+
+def fused_kernel(
+    tokens_ref, gain_ref, segments_ref, freq_ref, wq_ref, wkv_ref, wo_ref, out_ref,
+    tok_all, stats, normed, wq, wkv, wo, part, recv_a, sum_b, recv_b, final, mixed_send, mixed_all,
+    out_acc, out_part, out_recv_a, out_sum_b, out_recv_b,
+    local_sem, weight_sem,
+    tok_send, tok_recv, stat_send, stat_recv,
+    a_send, a_recv, b_send, b_recv, mix_send, mix_recv,
+    oa_send, oa_recv, ob_send, ob_recv,
+):
+    side = 4
+    gx = lax.axis_index("gx")
+    gy = lax.axis_index("gy")
+    chip, core = gy // 2, gy % 2
+    me = gx * side + gy
+    mate = {"gx": gx, "gy": chip * 2 + (1 - core)}
+    across = {"gx": gx, "gy": (1 - chip) * 2 + core}
+    rows = tok_all.shape[1]
+    width = tok_all.shape[2]
+    query_tiles = wq_ref.shape[1] // TILE
+    tiles = query_tiles + 1
+
+    own_tokens = pltpu.make_async_copy(tokens_ref, tok_all.at[gx], local_sem.at[0])
+    own_tokens.start()
+    weight_copies = [pltpu.make_async_copy(wkv_ref, wkv, weight_sem.at[0])]
+    for n in range(query_tiles):
+        cols = pl.ds(n * TILE, TILE)
+        weight_copies.append(
+            pltpu.make_async_copy(wq_ref.at[:, cols], wq.at[:, cols], weight_sem.at[1 + n])
+        )
+    half = wo_ref.shape[0] // 2
+    for j in range(2):
+        span = pl.ds(j * half, half)
+        weight_copies.append(
+            pltpu.make_async_copy(wo_ref.at[span, :], wo.at[span, :], weight_sem.at[tiles + j])
+        )
+    for copy in weight_copies:
+        copy.start()
+
+    barrier = pltpu.get_barrier_semaphore()
+    for step in range(1, side * side):
+        peer = (me + step) % (side * side)
+        pl.semaphore_signal(
+            barrier, inc=1, device_id={"gx": peer // side, "gy": peer % side}, device_id_type=MESH
+        )
+    own_tokens.wait()
+    mine = tok_all[gx].astype(jnp.float32)
+    square_sum = jnp.sum(mine * mine, axis=1, keepdims=True)
+    row_id = lax.broadcasted_iota(jnp.int32, (rows, 128), 0)
+    col_id = lax.broadcasted_iota(jnp.int32, (rows, 128), 1)
+    diagonal = row_id == col_id
+    stats[me, 0:1, :] = jnp.sum(jnp.where(diagonal, square_sum, 0.0), axis=0, keepdims=True)
+    stats[me, 1:2, :] = segments_ref[...].astype(jnp.float32)
+    pl.semaphore_wait(barrier, side * side - 1)
+
+    stat_copies = []
+    for step in range(1, side * side):
+        peer = (me + step) % (side * side)
+        copy = pltpu.make_async_remote_copy(
+            src_ref=stats.at[me], dst_ref=stats.at[me],
+            send_sem=stat_send.at[step - 1], recv_sem=stat_recv.at[step - 1],
+            device_id={"gx": peer // side, "gy": peer % side}, device_id_type=MESH,
+        )
+        copy.start()
+        stat_copies.append(copy)
+    tok_copies = []
+    for step in range(1, side):
+        copy = pltpu.make_async_remote_copy(
+            src_ref=tokens_ref, dst_ref=tok_all.at[gx],
+            send_sem=tok_send.at[step - 1], recv_sem=tok_recv.at[step - 1],
+            device_id={"gx": (gx + step) % side, "gy": gy}, device_id_type=MESH,
+        )
+        copy.start()
+        tok_copies.append(copy)
+
+    for copy in stat_copies:
+        copy.wait_recv()
+
+    def as_column(row):
+        return jnp.sum(jnp.where(diagonal, row, 0.0), axis=1, keepdims=True)
+
+    segment_row = stats[gy * side + gy, 1:2, :]
+    segment_col = as_column(segment_row)
+    in_request = col_id < rows
+    context = jnp.sum(
+        jnp.where(in_request & (segment_row < 0.5), 1.0, 0.0), axis=1, keepdims=True
+    )
+    first = jnp.sum(
+        jnp.where(in_request & (segment_row < segment_col), 1.0, 0.0), axis=1, keepdims=True
+    )
+    index = row_id[:, 0:1].astype(jnp.float32)
+    position = jnp.where(segment_col < 0.5, index, context + index - first)
+    angle = position * freq_ref[...]
+    cosine = jnp.cos(angle)
+    sine = jnp.where(col_id < HEAD_WIDTH // 2, -jnp.sin(angle), jnp.sin(angle))
+    visible = (col_id <= row_id) & ((segment_row == segment_col) | (segment_row < 0.5))
+    visible = jnp.where(visible, 1.0, 0.0)[:, :rows]
+    group_width = QUERY_HEADS // KEYVALUE_HEADS
+    visible_all = jnp.concatenate([visible] * group_width, axis=0) > 0.5
+
+    gain = gain_ref[...]
+    for step in range(side):
+        block = (gx + step) % side if step == 0 else (gx - step + side) % side
+        if step > 0:
+            tok_copies[step - 1].wait_recv()
+        total = stats[block * side, 0:1, :]
+        for k in range(1, side):
+            total = total + stats[block * side + k, 0:1, :]
+        scale = lax.rsqrt(as_column(total) / MODEL_WIDTH + EPSILON)
+        normed[block] = (tok_all[block].astype(jnp.float32) * scale * gain).astype(jnp.bfloat16)
+
+    def rotated(values):
+        return (values * cosine + pltpu.roll(values, HEAD_WIDTH // 2, 1) * sine).astype(
+            jnp.bfloat16
+        )
+
+    a_copies, b_copies = [], []
+
+    def project(n):
+        weight_copies[n].wait()
+        if n == 0:
+            weights = wkv[...]
+        else:
+            weights = wq[:, (n - 1) * TILE : n * TILE]
+        value = jnp.dot(
+            normed[...].reshape(side * rows, width), weights, preferred_element_type=jnp.float32
+        )
+        for r in range(side):
+            part[n, r % 2, r // 2] = value[r * rows : (r + 1) * rows]
+        copy = pltpu.make_async_remote_copy(
+            src_ref=part.at[n, 1 - core], dst_ref=recv_a.at[n],
+            send_sem=a_send.at[n], recv_sem=a_recv.at[n], device_id=mate, device_id_type=MESH,
+        )
+        copy.start()
+        a_copies.append(copy)
+
+    def pass_on(n):
+        a_copies[n].wait_recv()
+        sum_b[n] = part[n, core, 1 - chip] + recv_a[n, 1 - chip]
+        copy = pltpu.make_async_remote_copy(
+            src_ref=sum_b.at[n], dst_ref=recv_b.at[n],
+            send_sem=b_send.at[n], recv_sem=b_recv.at[n], device_id=across, device_id_type=MESH,
+        )
+        copy.start()
+        b_copies.append(copy)
+
+    def finish(n):
+        b_copies[n].wait_recv()
+        return part[n, core, chip] + recv_a[n, chip] + recv_b[n]
+
+    for n in range(tiles):
+        project(n)
+        if n > 0:
+            pass_on(n - 1)
+    pass_on(tiles - 1)
+
+    heads_in_tile = TILE // HEAD_WIDTH
+    keyval = finish(0)
+    local_kv = wkv_ref.shape[1] // (2 * HEAD_WIDTH)
+    mix_copies = []
+    for j in range(local_kv):
+        key_head = rotated(keyval[:, 2 * j * HEAD_WIDTH : (2 * j + 1) * HEAD_WIDTH])
+        value_head = keyval[:, (2 * j + 1) * HEAD_WIDTH : (2 * j + 2) * HEAD_WIDTH].astype(
+            jnp.bfloat16
+        )
+        queries = []
+        for t in range(group_width // heads_in_tile):
+            query_tile = finish(1 + j * (group_width // heads_in_tile) + t)
+            for h in range(heads_in_tile):
+                queries.append(rotated(query_tile[:, h * HEAD_WIDTH : (h + 1) * HEAD_WIDTH]))
+        query = jnp.concatenate(queries, axis=0)
+        scores = lax.dot_general(
+            query, key_head, (((1,), (1,)), ((), ())), preferred_element_type=jnp.float32
+        ) * (HEAD_WIDTH ** (-0.5))
+        scores = jnp.where(visible_all, scores, MASK_VALUE)
+        weights = jnp.exp(scores - jnp.max(scores, axis=1, keepdims=True))
+        probs = (weights / jnp.sum(weights, axis=1, keepdims=True)).astype(jnp.bfloat16)
+        mixed = jnp.dot(probs, value_head, preferred_element_type=jnp.float32).astype(jnp.bfloat16)
+        for h in range(group_width):
+            mixed_send[j, :, h * HEAD_WIDTH : (h + 1) * HEAD_WIDTH] = mixed[
+                h * rows : (h + 1) * rows
+            ]
+
+        @pl.when(gx == gy)
+        def _():
+            mixed_all[j, gy] = mixed_send[j]
+
+        for step in (3, 2, 1, 0):
+            copy = pltpu.make_async_remote_copy(
+                src_ref=mixed_send.at[j], dst_ref=mixed_all.at[j, gy],
+                send_sem=mix_send.at[j, step], recv_sem=mix_recv.at[j, gy],
+                device_id={"gx": (gx + step) % side, "gy": gx}, device_id_type=MESH,
+            )
+            if step == 0:
+                pl.when(gx != gy)(copy.start)
+            else:
+                copy.start()
+            mix_copies.append((step, copy))
+
+    def wait_mixed(j):
+        for step in range(side):
+            r = (gy + step) % side
+            copy = pltpu.make_async_remote_copy(
+                src_ref=mixed_send.at[j], dst_ref=mixed_all.at[j, r],
+                send_sem=mix_send.at[j, 0], recv_sem=mix_recv.at[j, r],
+                device_id=mate, device_id_type=MESH,
+            )
+            if step == 0:
+                pl.when(gx != gy)(copy.wait_recv)
+            else:
+                copy.wait_recv()
+
+    out_tiles = wo_ref.shape[1] // TILE
+    wait_mixed(0)
+    weight_copies[tiles].wait()
+    for n in range(out_tiles):
+        out_acc[n] = jnp.dot(
+            mixed_all[0].reshape(side * rows, half), wo[0:half, n * TILE : (n + 1) * TILE],
+            preferred_element_type=jnp.float32,
+        )
+    wait_mixed(1)
+    weight_copies[tiles + 1].wait()
+
+    oa_copies, ob_copies = [], []
+
+    def out_project(n):
+        value = out_acc[n] + jnp.dot(
+            mixed_all[1].reshape(side * rows, half), wo[half:, n * TILE : (n + 1) * TILE],
+            preferred_element_type=jnp.float32,
+        )
+        for r in range(side):
+            out_part[n, r % 2, r // 2] = value[r * rows : (r + 1) * rows]
+        copy = pltpu.make_async_remote_copy(
+            src_ref=out_part.at[n, 1 - core], dst_ref=out_recv_a.at[n],
+            send_sem=oa_send.at[n], recv_sem=oa_recv.at[n], device_id=mate, device_id_type=MESH,
+        )
+        copy.start()
+        oa_copies.append(copy)
+
+    def out_pass_on(n):
+        oa_copies[n].wait_recv()
+        out_sum_b[n] = out_part[n, core, 1 - chip] + out_recv_a[n, 1 - chip]
+        copy = pltpu.make_async_remote_copy(
+            src_ref=out_sum_b.at[n], dst_ref=out_recv_b.at[n],
+            send_sem=ob_send.at[n], recv_sem=ob_recv.at[n], device_id=across, device_id_type=MESH,
+        )
+        copy.start()
+        ob_copies.append(copy)
+
+    for n in range(out_tiles):
+        out_project(n)
+        if n > 0:
+            out_pass_on(n - 1)
+    out_pass_on(out_tiles - 1)
+    for n in range(out_tiles):
+        ob_copies[n].wait_recv()
+        out_ref[:, n * TILE : (n + 1) * TILE] = (
+            out_part[n, core, chip] + out_recv_a[n, chip] + out_recv_b[n]
+        ).astype(jnp.bfloat16)
+
+    for copy in stat_copies + tok_copies + a_copies + b_copies + oa_copies + ob_copies:
+        copy.wait_send()
+    for step, copy in mix_copies:
+        if step == 0:
+            pl.when(gx != gy)(copy.wait_send)
+        else:
+            copy.wait_send()
+
+
+def fused_on_device(tokens, norm_gain, w_query, keyvalue_weight, w_out, segment_ids):
+    rows, width = tokens.shape
+    side = lax.axis_size("gx")
+    frequency = ROPE_BASE ** (
+        -2.0 * jnp.arange(HEAD_WIDTH // 2, dtype=jnp.float32) / HEAD_WIDTH
+    )
+    frequency = jnp.concatenate([frequency, frequency])[None, :]
+    segments = jnp.pad(segment_ids, ((0, 0), (0, 128 - segment_ids.shape[1])))
+    query_tiles = w_query.shape[1] // TILE
+    tiles = query_tiles + 1
+    out_tiles = w_out.shape[1] // TILE
+    half = w_out.shape[0] // 2
+    f32, bf16 = jnp.float32, jnp.bfloat16
+    dma = pltpu.SemaphoreType.DMA
+    vmem = pl.BlockSpec(memory_space=pltpu.VMEM)
+    hbm = pl.BlockSpec(memory_space=pl.ANY)
+    return pl.pallas_call(
+        fused_kernel,
+        out_shape=jax.ShapeDtypeStruct((rows, w_out.shape[1]), bf16),
+        in_specs=[hbm, vmem, vmem, vmem, hbm, hbm, hbm],
+        out_specs=vmem,
+        scratch_shapes=[
+            pltpu.VMEM((side, rows, width), bf16),
+            pltpu.VMEM((side * side, 8, 128), f32),
+            pltpu.VMEM((side, rows, width), bf16),
+            pltpu.VMEM(w_query.shape, bf16),
+            pltpu.VMEM(keyvalue_weight.shape, bf16),
+            pltpu.VMEM(w_out.shape, bf16),
+            pltpu.VMEM((tiles, 2, 2, rows, TILE), f32),
+            pltpu.VMEM((tiles, 2, rows, TILE), f32),
+            pltpu.VMEM((tiles, rows, TILE), f32),
+            pltpu.VMEM((tiles, rows, TILE), f32),
+            pltpu.VMEM((tiles, rows, TILE), f32),
+            pltpu.VMEM((2, rows, half), bf16),
+            pltpu.VMEM((2, side, rows, half), bf16),
+            pltpu.VMEM((out_tiles, side * rows, TILE), f32),
+            pltpu.VMEM((out_tiles, 2, 2, rows, TILE), f32),
+            pltpu.VMEM((out_tiles, 2, rows, TILE), f32),
+            pltpu.VMEM((out_tiles, rows, TILE), f32),
+            pltpu.VMEM((out_tiles, rows, TILE), f32),
+            dma((1,)), dma((tiles + 2,)),
+            dma((side - 1,)), dma((side - 1,)),
+            dma((side * side - 1,)), dma((side * side - 1,)),
+            dma((tiles,)), dma((tiles,)), dma((tiles,)), dma((tiles,)),
+            dma((2, side)), dma((2, side)),
+            dma((out_tiles,)), dma((out_tiles,)), dma((out_tiles,)), dma((out_tiles,)),
+        ],
+        compiler_params=pltpu.CompilerParams(
+            collective_id=0, has_side_effects=True, vmem_limit_bytes=48 * 1024 * 1024
+        ),
+        cost_estimate=pl.CostEstimate(
+            flops=2 * side * rows * width * (w_query.shape[1] * 2 + keyvalue_weight.shape[1]),
+            bytes_accessed=2 * (w_query.size + keyvalue_weight.size + w_out.size),
+            transcendentals=0,
+        ),
+    )(tokens, norm_gain[None, :], segments, frequency, w_query, keyvalue_weight, w_out)
+
+
+def program_for(mesh):
+    if mesh.shape["gx"] == 4 and mesh.shape["gy"] == 4:
+        return fused_on_device
+    return on_device
+
+
 def solution(mesh):
     return jax.shard_map(
-        on_device,
+        program_for(mesh),
         mesh=mesh,
         in_specs=(
             P(("groups", "gx"), "gy"),

time: 150 us -> 40 us (0.27)
  waiting for transfers between devices: 71.4 us -> 0 us
  blocking collectives: 36.8 us -> 0 us
  Pallas kernels: 0 us -> 35.3 us
  matrix products: 13.6 us -> 0 us
  between operations: 13.6 us -> 0.01 us
  starting transfers between devices: 8.11 us -> 0 us
  other arithmetic: 4.85 us -> 0.09 us
  local copies, waits for them, and re-layouts: 0.85 us -> 4.42 us
    pallas_call x0 -> x1, Pallas kernels: none -> 35.3 us  [fused_on_device(): pl.pallas_call(fused_kernel, out_shape=jax.ShapeDtypeStruct((rows, w_out....]
    psum x1 -> x0, waiting for transfers between devices: 33.8 us -> none  [on_device(): query_sum, keyval_sum = lax.psum((query_part, keyval_part), 'gy')]
    all_gather x2 -> x0, blocking collectives: 28.5 us -> none  [the longest x1 14.4 us: on_device(): lax.all_gather(mixed, 'gx', axis=0, tiled=True)]
    reduce_scatter x1 -> x0, waiting for transfers between devices: 20.4 us -> none  [on_device(): lax.psum_scatter(output_terms, 'gy', scatter_dimension=0, tiled=True)]
    all_to_all x2 -> x0, waiting for transfers between devices: 17.2 us -> none  [the longest x1 11.3 us: on_device(): lax.all_to_all(query_sum, 'gx', split_axis=0, concat_axis=1, tiled=True)]
    dot_general x4 -> x0, matrix products: 13.2 us -> none  [the longest x1 5.78 us: on_device(): jnp.dot(piece_rows, w_query, preferred_element_type=jnp.float32)]
    psum x1 -> x0, blocking collectives: 8.34 us -> none  [on_device(): squares = lax.psum(jnp.sum(widened * widened, axis=1), 'gy')]
    all_to_all x2 -> x0, starting transfers between devices: 8.07 us -> none  [the longest x1 4.6 us: on_device(): lax.all_to_all(keyval_sum, 'gx', split_axis=0, concat_axis=1, tiled=True)]
  transfers between devices with their start and end apart: 4 -> 0, of which waited for: 4 -> 0; matrix products, arithmetic and copies ran while one was open for 1% -> 0% of each run, Pallas kernels for 0% -> 0%
where the time goes in v1:
time: 40 us; the launch traced here: 39.8 us
  Pallas kernels  35.3 us (88%)
  local copies, waits for them, and re-layouts  4.42 us (11%)
    pallas_call x1, Pallas kernels, fused_on_device(): pl.pallas_call(fused_kernel, out_shape=jax.ShapeDtypeStruct((rows, w_out....  35.3 us
    unnamed x7, local copies, waits for them, and re-layouts  3.76 us

profile of v1, /device:TPU:0, one launch (start us, length us, event | category | flops | bytes accessed | tf_op | source)
XLA Modules:
  0.0 39.8 jit_solution(13690079498871050066)
XLA Ops:
  0.0 0.7 %pad.4.segments_ref = s32[1,128]{1,0:T(1,128)S(1)} pad(s32[1,16]{1,0:T(1,128)} %param.11, s32[]{:T(128)} %constant.3.clone.1), padding=0_0x0_112 | pad | bytes 580 | tf_op jit(solution)/shard_map/jit(_pad)/pad | solution.py:396
  0.7 0.1 maximum_bitcast_fusion.freq_ref
  0.7 0.0 copy-start
  0.8 1.6 %copy-done = bf16[2048,512]{1,0:T(8,128)(2,1)S(1)} copy-done((bf16[2048,512]{1,0:T(8,128)(2,1)S(1)}, bf16[2048,512]{1,0:T(8,128)(2,1)}, u32[]{:S(2)}) %copy-start) | copy-done | bytes 2097176
  2.3 0.0 copy-start.1
  2.3 0.8 %copy-done.1 = bf16[16,2048]{1,0:T(8,128)(2,1)S(1)} copy-done((bf16[16,2048]{1,0:T(8,128)(2,1)S(1)}, bf16[16,2048]{1,0:T(8,128)(2,1)}, u32[]{:S(2)}) %copy-start.1) | copy-done | bytes 65560
  3.2 0.0 copy-start.2
  3.2 0.7 %copy-done.2 = f32[2048]{0:T(1024)S(1)} copy-done((f32[2048]{0:T(1024)S(1)}, f32[2048]{0:T(1024)}, u32[]{:S(2)}) %copy-start.2) | copy-done | bytes 8216
  3.9 35.3 %shard_map.64 = bf16[16,2048]{1,0:T(8,128)(2,1)S(1)} custom-call(bf16[16,2048]{1,0:T(8,128)(2,1)S(1)} %copy-done.1, f32[1,2048]{1,0:T(1,128)S(1)} %bitcast.3, s32[1,128]{1,0:T(1,128)S(1)} %pad.4.segments_ref, f32[1,128]{1,0:T(1,128)S(1)} %maximum_bitcast_fusion.freq_ref, bf16[2048,2048]{1,0:T(8,128)(2,1)} %wq_ref.1, bf16[2048,512]{1,0:T(8,128)(2,1)S(1)} %copy-done, ...), custom_call_target="tpu_custom_call" | custom-call | flops 1207959552 | bytes 18874368 | tf_op jit(solution)/shard_map/pallas_call | solution.py:405
  39.1 0.6 %copy.8 = bf16[16,2048]{1,0:T(8,128)(2,1)} copy(bf16[16,2048]{1,0:T(8,128)(2,1)S(1)} %shard_map.64) | data formatting | bytes 131072
  (1 shorter events, 0.0 us)
Async XLA Ops:
  0.7 1.6 %copy-start = (bf16[2048,512]{1,0:T(8,128)(2,1)S(1)}, bf16[2048,512]{1,0:T(8,128)(2,1)}, u32[]{:S(2)}) copy-start(bf16[2048,512]{1,0:T(8,128)(2,1)} %wkv_ref.1) | copy-start | bytes 6291460
  2.3 0.8 %copy-start.1 = (bf16[16,2048]{1,0:T(8,128)(2,1)S(1)}, bf16[16,2048]{1,0:T(8,128)(2,1)}, u32[]{:S(2)}) copy-start(bf16[16,2048]{1,0:T(8,128)(2,1)} %tokens_ref.1) | copy-start | bytes 196612
  3.2 0.7 %copy-start.2 = (f32[2048]{0:T(1024)S(1)}, f32[2048]{0:T(1024)}, u32[]{:S(2)}) copy-start(f32[2048]{0:T(1024)} %param.7) | copy-start | bytes 24580

commit v2 on v1

--- a/solution.py
+++ b/solution.py
@@ -1,4 +1,4 @@
-import functools
+import math
 
 import jax
 import jax.numpy as jnp
@@ -116,11 +116,12 @@
 
 MESH = pl.DeviceIdType.MESH
 TILE = 512
+CHUNKS = 4
 
 
 def fused_kernel(
-    tokens_ref, gain_ref, segments_ref, freq_ref, wq_ref, wkv_ref, wo_ref, out_ref,
-    tok_all, stats, normed, wq, wkv, wo, part, recv_a, sum_b, recv_b, final, mixed_send, mixed_all,
+    tokens_ref, gain_hbm, segments_hbm, wq_ref, wkv_ref, wo_ref, out_ref,
+    gain_ref, segments_ref, tok_all, stats, normed, wq, wkv, wo, part, recv_a, sum_b, recv_b, final, mixed_send, mixed_all,
     out_acc, out_part, out_recv_a, out_sum_b, out_recv_b,
     local_sem, weight_sem,
     tok_send, tok_recv, stat_send, stat_recv,
@@ -134,26 +135,39 @@
     me = gx * side + gy
     mate = {"gx": gx, "gy": chip * 2 + (1 - core)}
     across = {"gx": gx, "gy": (1 - chip) * 2 + core}
-    rows = tok_all.shape[1]
-    width = tok_all.shape[2]
+    rows = tok_all.shape[2]
+    span = tok_all.shape[3]
     query_tiles = wq_ref.shape[1] // TILE
     tiles = query_tiles + 1
 
-    own_tokens = pltpu.make_async_copy(tokens_ref, tok_all.at[gx], local_sem.at[0])
-    own_tokens.start()
-    weight_copies = [pltpu.make_async_copy(wkv_ref, wkv, weight_sem.at[0])]
-    for n in range(query_tiles):
-        cols = pl.ds(n * TILE, TILE)
+    own_tokens = [
+        pltpu.make_async_copy(
+            tokens_ref.at[:, pl.ds(c * span, span)], tok_all.at[c, gx], local_sem.at[2 + c]
+        )
+        for c in range(CHUNKS)
+    ]
+    for copy in own_tokens:
+        copy.start()
+    own_segments = pltpu.make_async_copy(segments_hbm, segments_ref, local_sem.at[0])
+    own_segments.start()
+    own_gain = pltpu.make_async_copy(gain_hbm, gain_ref, local_sem.at[1])
+    own_gain.start()
+    weight_copies = []
+    for c in range(CHUNKS):
+        piece = pl.ds(c * span, span)
         weight_copies.append(
-            pltpu.make_async_copy(wq_ref.at[:, cols], wq.at[:, cols], weight_sem.at[1 + n])
+            pltpu.make_async_copy(wkv_ref.at[piece, :], wkv.at[piece, :], weight_sem.at[2 * c])
+        )
+        weight_copies.append(
+            pltpu.make_async_copy(wq_ref.at[piece, :], wq.at[piece, :], weight_sem.at[2 * c + 1])
         )
     half = wo_ref.shape[0] // 2
     for j in range(2):
-        span = pl.ds(j * half, half)
+        piece = pl.ds(j * half, half)
         weight_copies.append(
-            pltpu.make_async_copy(wo_ref.at[span, :], wo.at[span, :], weight_sem.at[tiles + j])
-        )
-    for copy in weight_copies:
+            pltpu.make_async_copy(wo_ref.at[piece, :], wo.at[piece, :], weight_sem.at[2 * CHUNKS + j])
+        )
+    for copy in weight_copies[: 2 * CHUNKS]:
         copy.start()
 
     barrier = pltpu.get_barrier_semaphore()
@@ -162,14 +176,25 @@
         pl.semaphore_signal(
             barrier, inc=1, device_id={"gx": peer // side, "gy": peer % side}, device_id_type=MESH
         )
-    own_tokens.wait()
-    mine = tok_all[gx].astype(jnp.float32)
-    square_sum = jnp.sum(mine * mine, axis=1, keepdims=True)
+    square_sum = jnp.zeros((rows, 1), jnp.float32)
+    for c in range(CHUNKS):
+        own_tokens[c].wait()
+        mine = tok_all[c, gx].astype(jnp.float32)
+        square_sum += jnp.sum(mine * mine, axis=1, keepdims=True)
     row_id = lax.broadcasted_iota(jnp.int32, (rows, 128), 0)
     col_id = lax.broadcasted_iota(jnp.int32, (rows, 128), 1)
     diagonal = row_id == col_id
+    stats[me] = jnp.zeros(stats.shape[1:], jnp.float32)
     stats[me, 0:1, :] = jnp.sum(jnp.where(diagonal, square_sum, 0.0), axis=0, keepdims=True)
-    stats[me, 1:2, :] = segments_ref[...].astype(jnp.float32)
+    own_segments.wait()
+    stats[me, 1:2, 0:rows] = segments_ref[...].astype(jnp.float32)
+    half_index = (col_id % (HEAD_WIDTH // 2)).astype(jnp.float32)
+    table_angle = row_id.astype(jnp.float32) * jnp.exp(
+        half_index * (-2.0 * math.log(ROPE_BASE) / HEAD_WIDTH)
+    )
+    cosine_table = jnp.cos(table_angle)
+    sine_table = jnp.sin(table_angle)
+    sine_table = jnp.where(col_id < HEAD_WIDTH // 2, -sine_table, sine_table)
     pl.semaphore_wait(barrier, side * side - 1)
 
     stat_copies = []
@@ -182,15 +207,30 @@
         )
         copy.start()
         stat_copies.append(copy)
-    tok_copies = []
-    for step in range(1, side):
-        copy = pltpu.make_async_remote_copy(
-            src_ref=tokens_ref, dst_ref=tok_all.at[gx],
-            send_sem=tok_send.at[step - 1], recv_sem=tok_recv.at[step - 1],
-            device_id={"gx": (gx + step) % side, "gy": gy}, device_id_type=MESH,
-        )
-        copy.start()
-        tok_copies.append(copy)
+    middle = (gx == 1) | (gx == 2)
+    outer = 3 * (gx // 2)
+    far = 3 - outer
+
+    def token_copy(c, slot, block, target):
+        return pltpu.make_async_remote_copy(
+            src_ref=tok_all.at[c, block], dst_ref=tok_all.at[c, block],
+            send_sem=tok_send.at[c, slot], recv_sem=tok_recv.at[c, block],
+            device_id={"gx": target, "gy": gy}, device_id_type=MESH,
+        )
+
+    for c in range(CHUNKS):
+        token_copy(c, 1, gx, (gx + 2) % side).start()
+        token_copy(c, 0, gx, 1 + gx % 2).start()
+        pl.when(middle)(token_copy(c, 2, gx, outer).start)
+    for copy in weight_copies[2 * CHUNKS :]:
+        copy.start()
+
+    def hand_on(c):
+        @pl.when(middle)
+        def _():
+            copy = token_copy(c, 3, far, outer)
+            copy.wait_recv()
+            copy.start()
 
     for copy in stat_copies:
         copy.wait_recv()
@@ -209,24 +249,24 @@
     )
     index = row_id[:, 0:1].astype(jnp.float32)
     position = jnp.where(segment_col < 0.5, index, context + index - first)
-    angle = position * freq_ref[...]
-    cosine = jnp.cos(angle)
-    sine = jnp.where(col_id < HEAD_WIDTH // 2, -jnp.sin(angle), jnp.sin(angle))
+    cosine = jnp.zeros((rows, HEAD_WIDTH), jnp.float32)
+    sine = jnp.zeros((rows, HEAD_WIDTH), jnp.float32)
+    for p in range(rows):
+        here = position == float(p)
+        cosine = jnp.where(here, cosine_table[p : p + 1], cosine)
+        sine = jnp.where(here, sine_table[p : p + 1], sine)
     visible = (col_id <= row_id) & ((segment_row == segment_col) | (segment_row < 0.5))
     visible = jnp.where(visible, 1.0, 0.0)[:, :rows]
     group_width = QUERY_HEADS // KEYVALUE_HEADS
     visible_all = jnp.concatenate([visible] * group_width, axis=0) > 0.5
 
-    gain = gain_ref[...]
-    for step in range(side):
-        block = (gx + step) % side if step == 0 else (gx - step + side) % side
-        if step > 0:
-            tok_copies[step - 1].wait_recv()
+    own_gain.wait()
+    scales = []
+    for block in range(side):
         total = stats[block * side, 0:1, :]
         for k in range(1, side):
             total = total + stats[block * side + k, 0:1, :]
-        scale = lax.rsqrt(as_column(total) / MODEL_WIDTH + EPSILON)
-        normed[block] = (tok_all[block].astype(jnp.float32) * scale * gain).astype(jnp.bfloat16)
+        scales.append(lax.rsqrt(as_column(total) / MODEL_WIDTH + EPSILON))
 
     def rotated(values):
         return (values * cosine + pltpu.roll(values, HEAD_WIDTH // 2, 1) * sine).astype(
@@ -235,17 +275,32 @@
 
     a_copies, b_copies = [], []
 
-    def project(n):
-        weight_copies[n].wait()
-        if n == 0:
-            weights = wkv[...]
-        else:
-            weights = wq[:, (n - 1) * TILE : n * TILE]
+    def normalize(c):
+        for step in (1, 3, 2):
+            copy = token_copy(c, 0, (gx + step) % side, outer)
+            if step == 2:
+                pl.when(jnp.logical_not(middle))(copy.wait_recv)
+            else:
+                copy.wait_recv()
+        gain = gain_ref[:, c * span : (c + 1) * span]
+        for block in range(side):
+            normed[c, block] = (
+                tok_all[c, block].astype(jnp.float32) * scales[block] * gain
+            ).astype(jnp.bfloat16)
+        weight_copies[2 * c].wait()
+        weight_copies[2 * c + 1].wait()
+
+    def project(c, n):
+        piece = slice(c * span, (c + 1) * span)
+        weights = wkv[piece, :] if n == 0 else wq[piece, (n - 1) * TILE : n * TILE]
         value = jnp.dot(
-            normed[...].reshape(side * rows, width), weights, preferred_element_type=jnp.float32
+            normed[c].reshape(side * rows, span), weights, preferred_element_type=jnp.float32
         )
         for r in range(side):
-            part[n, r % 2, r // 2] = value[r * rows : (r + 1) * rows]
+            term = value[r * rows : (r + 1) * rows]
+            part[n, r % 2, r // 2] = term if c == 0 else part[n, r % 2, r // 2] + term
+
+    def give_mate(n):
         copy = pltpu.make_async_remote_copy(
             src_ref=part.at[n, 1 - core], dst_ref=recv_a.at[n],
             send_sem=a_send.at[n], recv_sem=a_recv.at[n], device_id=mate, device_id_type=MESH,
@@ -267,8 +322,16 @@
         b_copies[n].wait_recv()
         return part[n, core, chip] + recv_a[n, chip] + recv_b[n]
 
+    hand_on(0)
+    for c in range(CHUNKS - 1):
+        hand_on(c + 1)
+        normalize(c)
+        for n in range(tiles):
+            project(c, n)
+    normalize(CHUNKS - 1)
     for n in range(tiles):
-        project(n)
+        project(CHUNKS - 1, n)
+        give_mate(n)
         if n > 0:
             pass_on(n - 1)
     pass_on(tiles - 1)
@@ -331,14 +394,14 @@
 
     out_tiles = wo_ref.shape[1] // TILE
     wait_mixed(0)
-    weight_copies[tiles].wait()
+    weight_copies[2 * CHUNKS].wait()
     for n in range(out_tiles):
         out_acc[n] = jnp.dot(
             mixed_all[0].reshape(side * rows, half), wo[0:half, n * TILE : (n + 1) * TILE],
             preferred_element_type=jnp.float32,
         )
     wait_mixed(1)
-    weight_copies[tiles + 1].wait()
+    weight_copies[2 * CHUNKS + 1].wait()
 
     oa_copies, ob_copies = [], []
 
@@ -377,7 +440,16 @@
             out_part[n, core, chip] + out_recv_a[n, chip] + out_recv_b[n]
         ).astype(jnp.bfloat16)
 
-    for copy in stat_copies + tok_copies + a_copies + b_copies + oa_copies + ob_copies:
+    for c in range(CHUNKS):
+        token_copy(c, 0, gx, outer).wait_send()
+        token_copy(c, 1, gx, outer).wait_send()
+
+        @pl.when(middle)
+        def _():
+            token_copy(c, 2, gx, outer).wait_send()
+            token_copy(c, 3, far, outer).wait_send()
+
+    for copy in stat_copies + a_copies + b_copies + oa_copies + ob_copies:
         copy.wait_send()
     for step, copy in mix_copies:
         if step == 0:
@@ -389,11 +461,6 @@
 def fused_on_device(tokens, norm_gain, w_query, keyvalue_weight, w_out, segment_ids):
     rows, width = tokens.shape
     side = lax.axis_size("gx")
-    frequency = ROPE_BASE ** (
-        -2.0 * jnp.arange(HEAD_WIDTH // 2, dtype=jnp.float32) / HEAD_WIDTH
-    )
-    frequency = jnp.concatenate([frequency, frequency])[None, :]
-    segments = jnp.pad(segment_ids, ((0, 0), (0, 128 - segment_ids.shape[1])))
     query_tiles = w_query.shape[1] // TILE
     tiles = query_tiles + 1
     out_tiles = w_out.shape[1] // TILE
@@ -405,12 +472,14 @@
     return pl.pallas_call(
         fused_kernel,
         out_shape=jax.ShapeDtypeStruct((rows, w_out.shape[1]), bf16),
-        in_specs=[hbm, vmem, vmem, vmem, hbm, hbm, hbm],
+        in_specs=[hbm] * 6,
         out_specs=vmem,
         scratch_shapes=[
-            pltpu.VMEM((side, rows, width), bf16),
+            pltpu.VMEM((1, width), f32),
+            pltpu.VMEM(segment_ids.shape, jnp.int32),
+            pltpu.VMEM((CHUNKS, side, rows, width // CHUNKS), bf16),
             pltpu.VMEM((side * side, 8, 128), f32),
-            pltpu.VMEM((side, rows, width), bf16),
+            pltpu.VMEM((CHUNKS, side, rows, width // CHUNKS), bf16),
             pltpu.VMEM(w_query.shape, bf16),
             pltpu.VMEM(keyvalue_weight.shape, bf16),
             pltpu.VMEM(w_out.shape, bf16),
@@ -426,22 +495,22 @@
             pltpu.VMEM((out_tiles, 2, rows, TILE), f32),
             pltpu.VMEM((out_tiles, rows, TILE), f32),
             pltpu.VMEM((out_tiles, rows, TILE), f32),
-            dma((1,)), dma((tiles + 2,)),
-            dma((side - 1,)), dma((side - 1,)),
+            dma((2 + CHUNKS,)), dma((2 * CHUNKS + 2,)),
+            dma((CHUNKS, side)), dma((CHUNKS, side)),
             dma((side * side - 1,)), dma((side * side - 1,)),
             dma((tiles,)), dma((tiles,)), dma((tiles,)), dma((tiles,)),
             dma((2, side)), dma((2, side)),
             dma((out_tiles,)), dma((out_tiles,)), dma((out_tiles,)), dma((out_tiles,)),
         ],
         compiler_params=pltpu.CompilerParams(
-            collective_id=0, has_side_effects=True, vmem_limit_bytes=48 * 1024 * 1024
+            collective_id=0, has_side_effects=True, vmem_limit_bytes=63 * 1024 * 1024
         ),
         cost_estimate=pl.CostEstimate(
             flops=2 * side * rows * width * (w_query.shape[1] * 2 + keyvalue_weight.shape[1]),
             bytes_accessed=2 * (w_query.size + keyvalue_weight.size + w_out.size),
             transcendentals=0,
         ),
-    )(tokens, norm_gain[None, :], segments, frequency, w_query, keyvalue_weight, w_out)
+    )(tokens, norm_gain[None, :], segment_ids, w_query, keyvalue_weight, w_out)
 
 
 def program_for(mesh):

time: 40 us -> 37.3 us (0.932)
  local copies, waits for them, and re-layouts: 4.42 us -> 1.47 us
  Pallas kernels: 35.3 us -> 35.7 us
    unnamed x7 -> x1, local copies, waits for them, and re-layouts: 3.76 us -> 1.47 us
    pad x1 -> x0, local copies, waits for them, and re-layouts: 0.66 us -> none  [fused_on_device(): segments = jnp.pad(segment_ids, ((0, 0), (0, 128 - segment_ids.shape[1])))]
    pallas_call x1, Pallas kernels: 35.3 us -> 35.7 us  [fused_on_device(): pl.pallas_call(fused_kernel, out_shape=jax.ShapeDtypeStruct((rows, w_out....]
where the time goes in v2:
time: 37.3 us; the launch traced here: 37.2 us
  Pallas kernels  35.7 us (96%)
  local copies, waits for them, and re-layouts  1.47 us (4%)
    pallas_call x1, Pallas kernels, fused_on_device(): pl.pallas_call(fused_kernel, out_shape=jax.ShapeDtypeStruct((rows, w_out....  35.7 us
    unnamed x1, local copies, waits for them, and re-layouts  1.47 us

profile of v2, /device:TPU:0, one launch (start us, length us, event | category | flops | bytes accessed | tf_op | source)
XLA Modules:
  0.0 37.2 jit_solution(16598045316556455620)
XLA Ops:
  0.0 35.7 %shard_map.64 = bf16[16,2048]{1,0:T(8,128)(2,1)} custom-call(bf16[16,2048]{1,0:T(8,128)(2,1)} %tokens_ref.1, f32[1,2048]{1,0:T(1,128)} %bitcast.1, s32[1,16]{1,0:T(1,128)} %segments_hbm.1, bf16[2048,2048]{1,0:T(8,128)(2,1)} %wq_ref.1, bf16[2048,512]{1,0:T(8,128)(2,1)} %wkv_ref.1, bf16[2048,2048]{1,0:T(8,128)(2,1)} %wo_ref.1), custom_call_target="tpu_custom_call" | custom-call | flops 1207959552 | bytes 18874368 | tf_op jit(solution)/shard_map/pallas_call | solution.py:472
  35.7 1.5 %copy.8 = bf16[16,2048]{1,0:T(8,128)(2,1)} copy(bf16[16,2048]{1,0:T(8,128)(2,1)} %shard_map.64) | data formatting | bytes 131072

commit v3 on v2

--- a/solution.py
+++ b/solution.py
@@ -116,7 +116,7 @@
 
 MESH = pl.DeviceIdType.MESH
 TILE = 512
-CHUNKS = 4
+CHUNKS = 2
 
 
 def fused_kernel(
@@ -258,7 +258,7 @@
     visible = (col_id <= row_id) & ((segment_row == segment_col) | (segment_row < 0.5))
     visible = jnp.where(visible, 1.0, 0.0)[:, :rows]
     group_width = QUERY_HEADS // KEYVALUE_HEADS
-    visible_all = jnp.concatenate([visible] * group_width, axis=0) > 0.5
+    visible_all = jnp.concatenate([visible] * (TILE // HEAD_WIDTH), axis=0) > 0.5
 
     own_gain.wait()
     scales = []
@@ -332,25 +332,30 @@
     for n in range(tiles):
         project(CHUNKS - 1, n)
         give_mate(n)
-        if n > 0:
-            pass_on(n - 1)
-    pass_on(tiles - 1)
+        if n > 2:
+            pass_on(n - 3)
+    for n in range(tiles - 3, tiles):
+        pass_on(n)
 
     heads_in_tile = TILE // HEAD_WIDTH
     keyval = finish(0)
-    local_kv = wkv_ref.shape[1] // (2 * HEAD_WIDTH)
     mix_copies = []
-    for j in range(local_kv):
-        key_head = rotated(keyval[:, 2 * j * HEAD_WIDTH : (2 * j + 1) * HEAD_WIDTH])
-        value_head = keyval[:, (2 * j + 1) * HEAD_WIDTH : (2 * j + 2) * HEAD_WIDTH].astype(
-            jnp.bfloat16
-        )
-        queries = []
-        for t in range(group_width // heads_in_tile):
-            query_tile = finish(1 + j * (group_width // heads_in_tile) + t)
-            for h in range(heads_in_tile):
-                queries.append(rotated(query_tile[:, h * HEAD_WIDTH : (h + 1) * HEAD_WIDTH]))
-        query = jnp.concatenate(queries, axis=0)
+    key_head = value_head = None
+    for t in range(query_tiles):
+        if t * heads_in_tile % group_width == 0:
+            j = t * heads_in_tile // group_width
+            key_head = rotated(keyval[:, 2 * j * HEAD_WIDTH : (2 * j + 1) * HEAD_WIDTH])
+            value_head = keyval[:, (2 * j + 1) * HEAD_WIDTH : (2 * j + 2) * HEAD_WIDTH].astype(
+                jnp.bfloat16
+            )
+        query_tile = finish(1 + t)
+        query = jnp.concatenate(
+            [
+                rotated(query_tile[:, h * HEAD_WIDTH : (h + 1) * HEAD_WIDTH])
+                for h in range(heads_in_tile)
+            ],
+            axis=0,
+        )
         scores = lax.dot_general(
             query, key_head, (((1,), (1,)), ((), ())), preferred_element_type=jnp.float32
         ) * (HEAD_WIDTH ** (-0.5))
@@ -358,19 +363,19 @@
         weights = jnp.exp(scores - jnp.max(scores, axis=1, keepdims=True))
         probs = (weights / jnp.sum(weights, axis=1, keepdims=True)).astype(jnp.bfloat16)
         mixed = jnp.dot(probs, value_head, preferred_element_type=jnp.float32).astype(jnp.bfloat16)
-        for h in range(group_width):
-            mixed_send[j, :, h * HEAD_WIDTH : (h + 1) * HEAD_WIDTH] = mixed[
+        for h in range(heads_in_tile):
+            mixed_send[t, :, h * HEAD_WIDTH : (h + 1) * HEAD_WIDTH] = mixed[
                 h * rows : (h + 1) * rows
             ]
 
         @pl.when(gx == gy)
         def _():
-            mixed_all[j, gy] = mixed_send[j]
+            mixed_all[t, gy] = mixed_send[t]
 
         for step in (3, 2, 1, 0):
             copy = pltpu.make_async_remote_copy(
-                src_ref=mixed_send.at[j], dst_ref=mixed_all.at[j, gy],
-                send_sem=mix_send.at[j, step], recv_sem=mix_recv.at[j, gy],
+                src_ref=mixed_send.at[t], dst_ref=mixed_all.at[t, gy],
+                send_sem=mix_send.at[t, step], recv_sem=mix_recv.at[t, gy],
                 device_id={"gx": (gx + step) % side, "gy": gx}, device_id_type=MESH,
             )
             if step == 0:
@@ -379,12 +384,12 @@
                 copy.start()
             mix_copies.append((step, copy))
 
-    def wait_mixed(j):
+    def wait_mixed(t):
         for step in range(side):
             r = (gy + step) % side
             copy = pltpu.make_async_remote_copy(
-                src_ref=mixed_send.at[j], dst_ref=mixed_all.at[j, r],
-                send_sem=mix_send.at[j, 0], recv_sem=mix_recv.at[j, r],
+                src_ref=mixed_send.at[t], dst_ref=mixed_all.at[t, r],
+                send_sem=mix_send.at[t, 0], recv_sem=mix_recv.at[t, r],
                 device_id=mate, device_id_type=MESH,
             )
             if step == 0:
@@ -393,23 +398,28 @@
                 copy.wait_recv()
 
     out_tiles = wo_ref.shape[1] // TILE
-    wait_mixed(0)
-    weight_copies[2 * CHUNKS].wait()
-    for n in range(out_tiles):
-        out_acc[n] = jnp.dot(
-            mixed_all[0].reshape(side * rows, half), wo[0:half, n * TILE : (n + 1) * TILE],
+
+    def out_term(t, n):
+        return jnp.dot(
+            mixed_all[t].reshape(side * rows, TILE),
+            wo[t * TILE : (t + 1) * TILE, n * TILE : (n + 1) * TILE],
             preferred_element_type=jnp.float32,
         )
-    wait_mixed(1)
-    weight_copies[2 * CHUNKS + 1].wait()
+
+    for t in range(query_tiles - 1):
+        wait_mixed(t)
+        if t == 0:
+            weight_copies[2 * CHUNKS].wait()
+        if t == query_tiles // 2:
+            weight_copies[2 * CHUNKS + 1].wait()
+        for n in range(out_tiles):
+            out_acc[n] = out_term(t, n) if t == 0 else out_acc[n] + out_term(t, n)
+    wait_mixed(query_tiles - 1)
 
     oa_copies, ob_copies = [], []
 
     def out_project(n):
-        value = out_acc[n] + jnp.dot(
-            mixed_all[1].reshape(side * rows, half), wo[half:, n * TILE : (n + 1) * TILE],
-            preferred_element_type=jnp.float32,
-        )
+        value = out_acc[n] + out_term(query_tiles - 1, n)
         for r in range(side):
             out_part[n, r % 2, r // 2] = value[r * rows : (r + 1) * rows]
         copy = pltpu.make_async_remote_copy(
@@ -431,9 +441,10 @@
 
     for n in range(out_tiles):
         out_project(n)
-        if n > 0:
-            out_pass_on(n - 1)
-    out_pass_on(out_tiles - 1)
+        if n > 1:
+            out_pass_on(n - 2)
+    for n in range(out_tiles - 2, out_tiles):
+        out_pass_on(n)
     for n in range(out_tiles):
         ob_copies[n].wait_recv()
         out_ref[:, n * TILE : (n + 1) * TILE] = (
@@ -464,7 +475,6 @@
     query_tiles = w_query.shape[1] // TILE
     tiles = query_tiles + 1
     out_tiles = w_out.shape[1] // TILE
-    half = w_out.shape[0] // 2
     f32, bf16 = jnp.float32, jnp.bfloat16
     dma = pltpu.SemaphoreType.DMA
     vmem = pl.BlockSpec(memory_space=pltpu.VMEM)
@@ -488,8 +498,8 @@
             pltpu.VMEM((tiles, rows, TILE), f32),
             pltpu.VMEM((tiles, rows, TILE), f32),
             pltpu.VMEM((tiles, rows, TILE), f32),
-            pltpu.VMEM((2, rows, half), bf16),
-            pltpu.VMEM((2, side, rows, half), bf16),
+            pltpu.VMEM((query_tiles, rows, TILE), bf16),
+            pltpu.VMEM((query_tiles, side, rows, TILE), bf16),
             pltpu.VMEM((out_tiles, side * rows, TILE), f32),
             pltpu.VMEM((out_tiles, 2, 2, rows, TILE), f32),
             pltpu.VMEM((out_tiles, 2, rows, TILE), f32),
@@ -499,7 +509,7 @@
             dma((CHUNKS, side)), dma((CHUNKS, side)),
             dma((side * side - 1,)), dma((side * side - 1,)),
             dma((tiles,)), dma((tiles,)), dma((tiles,)), dma((tiles,)),
-            dma((2, side)), dma((2, side)),
+            dma((query_tiles, side)), dma((query_tiles, side)),
             dma((out_tiles,)), dma((out_tiles,)), dma((out_tiles,)), dma((out_tiles,)),
         ],
         compiler_params=pltpu.CompilerParams(

time: 37.3 us -> 36.4 us (0.976)
  Pallas kernels: 35.7 us -> 34.8 us
    pallas_call x1, Pallas kernels: 35.7 us -> 34.8 us  [fused_on_device(): pl.pallas_call(fused_kernel, out_shape=jax.ShapeDtypeStruct((rows, w_out....]
where the time goes in v3:
time: 36.4 us; the launch traced here: 36.3 us
  Pallas kernels  34.8 us (96%)
  local copies, waits for them, and re-layouts  1.47 us (4%)
    pallas_call x1, Pallas kernels, fused_on_device(): pl.pallas_call(fused_kernel, out_shape=jax.ShapeDtypeStruct((rows, w_out....  34.8 us
    unnamed x1, local copies, waits for them, and re-layouts  1.47 us

profile of v3, /device:TPU:0, one launch (start us, length us, event | category | flops | bytes accessed | tf_op | source)
XLA Modules:
  0.0 36.3 jit_solution(11268046933978503320)
XLA Ops:
  0.0 34.8 %shard_map.64 = bf16[16,2048]{1,0:T(8,128)(2,1)} custom-call(bf16[16,2048]{1,0:T(8,128)(2,1)} %tokens_ref.1, f32[1,2048]{1,0:T(1,128)} %bitcast.1, s32[1,16]{1,0:T(1,128)} %segments_hbm.1, bf16[2048,2048]{1,0:T(8,128)(2,1)} %wq_ref.1, bf16[2048,512]{1,0:T(8,128)(2,1)} %wkv_ref.1, bf16[2048,2048]{1,0:T(8,128)(2,1)} %wo_ref.1), custom_call_target="tpu_custom_call" | custom-call | flops 1207959552 | bytes 18874368 | tf_op jit(solution)/shard_map/pallas_call | solution.py:482
  34.8 1.5 %copy.8 = bf16[16,2048]{1,0:T(8,128)(2,1)} copy(bf16[16,2048]{1,0:T(8,128)(2,1)} %shard_map.64) | data formatting | bytes 131072

commit v4 on v3

--- a/solution.py
+++ b/solution.py
@@ -123,6 +123,7 @@
     tokens_ref, gain_hbm, segments_hbm, wq_ref, wkv_ref, wo_ref, out_ref,
     gain_ref, segments_ref, tok_all, stats, normed, wq, wkv, wo, part, recv_a, sum_b, recv_b, final, mixed_send, mixed_all,
     out_acc, out_part, out_recv_a, out_sum_b, out_recv_b,
+    first_recv, first_sem, out_first_recv, out_first_sem,
     local_sem, weight_sem,
     tok_send, tok_recv, stat_send, stat_recv,
     a_send, a_recv, b_send, b_recv, mix_send, mix_recv,
@@ -273,7 +274,7 @@
             jnp.bfloat16
         )
 
-    a_copies, b_copies = [], []
+    a_copies, b_copies, first_copies = [None], [None], []
 
     def normalize(c):
         for step in (1, 3, 2):
@@ -300,6 +301,22 @@
             term = value[r * rows : (r + 1) * rows]
             part[n, r % 2, r // 2] = term if c == 0 else part[n, r % 2, r // 2] + term
 
+    diagonal_peer = {"gx": gx, "gy": (1 - chip) * 2 + (1 - core)}
+    owners = [(mate, 1 - core, chip), (across, core, 1 - chip), (diagonal_peer, 1 - core, 1 - chip)]
+
+    def give_owners(source, landing, send_sem, recv_sem):
+        copies = []
+        for k in (1, 2, 0):
+            peer, peer_core, peer_chip = owners[k]
+            copy = pltpu.make_async_remote_copy(
+                src_ref=source.at[peer_core, peer_chip], dst_ref=landing.at[k],
+                send_sem=send_sem.at[k], recv_sem=recv_sem.at[k],
+                device_id=peer, device_id_type=MESH,
+            )
+            copy.start()
+            copies.append(copy)
+        return copies
+
     def give_mate(n):
         copy = pltpu.make_async_remote_copy(
             src_ref=part.at[n, 1 - core], dst_ref=recv_a.at[n],
@@ -319,6 +336,10 @@
         b_copies.append(copy)
 
     def finish(n):
+        if n == 0:
+            for copy in first_copies:
+                copy.wait_recv()
+            return part[0, core, chip] + first_recv[0] + (first_recv[1] + first_recv[2])
         b_copies[n].wait_recv()
         return part[n, core, chip] + recv_a[n, chip] + recv_b[n]
 
@@ -331,8 +352,11 @@
     normalize(CHUNKS - 1)
     for n in range(tiles):
         project(CHUNKS - 1, n)
-        give_mate(n)
-        if n > 2:
+        if n == 0:
+            first_copies.extend(give_owners(part.at[0], first_recv, first_sem.at[0], first_sem.at[1]))
+        else:
+            give_mate(n)
+        if n > 3:
             pass_on(n - 3)
     for n in range(tiles - 3, tiles):
         pass_on(n)
@@ -416,12 +440,19 @@
             out_acc[n] = out_term(t, n) if t == 0 else out_acc[n] + out_term(t, n)
     wait_mixed(query_tiles - 1)
 
-    oa_copies, ob_copies = [], []
+    oa_copies, ob_copies, out_first_copies = [], [], []
 
     def out_project(n):
         value = out_acc[n] + out_term(query_tiles - 1, n)
         for r in range(side):
             out_part[n, r % 2, r // 2] = value[r * rows : (r + 1) * rows]
+        if n == 0:
+            out_first_copies.extend(
+                give_owners(out_part.at[0], out_first_recv, out_first_sem.at[0], out_first_sem.at[1])
+            )
+            oa_copies.append(None)
+            ob_copies.append(None)
+            return
         copy = pltpu.make_async_remote_copy(
             src_ref=out_part.at[n, 1 - core], dst_ref=out_recv_a.at[n],
             send_sem=oa_send.at[n], recv_sem=oa_recv.at[n], device_id=mate, device_id_type=MESH,
@@ -441,11 +472,16 @@
 
     for n in range(out_tiles):
         out_project(n)
-        if n > 1:
+        if n > 2:
             out_pass_on(n - 2)
     for n in range(out_tiles - 2, out_tiles):
         out_pass_on(n)
-    for n in range(out_tiles):
+    for copy in out_first_copies:
+        copy.wait_recv()
+    out_ref[:, 0:TILE] = (
+        out_part[0, core, chip] + out_first_recv[0] + (out_first_recv[1] + out_first_recv[2])
+    ).astype(jnp.bfloat16)
+    for n in range(1, out_tiles):
         ob_copies[n].wait_recv()
         out_ref[:, n * TILE : (n + 1) * TILE] = (
             out_part[n, core, chip] + out_recv_a[n, chip] + out_recv_b[n]
@@ -460,7 +496,9 @@
             token_copy(c, 2, gx, outer).wait_send()
             token_copy(c, 3, far, outer).wait_send()
 
-    for copy in stat_copies + a_copies + b_copies + oa_copies + ob_copies:
+    for copy in stat_copies + first_copies + a_copies[1:] + b_copies[1:]:
+        copy.wait_send()
+    for copy in out_first_copies + oa_copies[1:] + ob_copies[1:]:
         copy.wait_send()
     for step, copy in mix_copies:
         if step == 0:
@@ -488,7 +526,7 @@
             pltpu.VMEM((1, width), f32),
             pltpu.VMEM(segment_ids.shape, jnp.int32),
             pltpu.VMEM((CHUNKS, side, rows, width // CHUNKS), bf16),
-            pltpu.VMEM((side * side, 8, 128), f32),
+            pltpu.VMEM((side * side, 2, 128), f32),
             pltpu.VMEM((CHUNKS, side, rows, width // CHUNKS), bf16),
             pltpu.VMEM(w_query.shape, bf16),
             pltpu.VMEM(keyvalue_weight.shape, bf16),
@@ -505,6 +543,10 @@
             pltpu.VMEM((out_tiles, 2, rows, TILE), f32),
             pltpu.VMEM((out_tiles, rows, TILE), f32),
             pltpu.VMEM((out_tiles, rows, TILE), f32),
+            pltpu.VMEM((3, rows, TILE), f32),
+            dma((2, 3)),
+            pltpu.VMEM((3, rows, TILE), f32),
+            dma((2, 3)),
             dma((2 + CHUNKS,)), dma((2 * CHUNKS + 2,)),
             dma((CHUNKS, side)), dma((CHUNKS, side)),
             dma((side * side - 1,)), dma((side * side - 1,)),

time: 36.4 us -> 35.1 us (0.964)
  Pallas kernels: 34.8 us -> 33.5 us
    pallas_call x1, Pallas kernels: 34.8 us -> 33.5 us  [fused_on_device(): pl.pallas_call(fused_kernel, out_shape=jax.ShapeDtypeStruct((rows, w_out....]
where the time goes in v4:
time: 35.1 us; the launch traced here: 35 us
  Pallas kernels  33.5 us (95%)
  local copies, waits for them, and re-layouts  1.47 us (4%)
    pallas_call x1, Pallas kernels, fused_on_device(): pl.pallas_call(fused_kernel, out_shape=jax.ShapeDtypeStruct((rows, w_out....  33.5 us
    unnamed x1, local copies, waits for them, and re-layouts  1.47 us

profile of v4, /device:TPU:0, one launch (start us, length us, event | category | flops | bytes accessed | tf_op | source)
XLA Modules:
  0.0 35.0 jit_solution(4404946046136648030)
XLA Ops:
  0.0 33.5 %shard_map.64 = bf16[16,2048]{1,0:T(8,128)(2,1)} custom-call(bf16[16,2048]{1,0:T(8,128)(2,1)} %tokens_ref.1, f32[1,2048]{1,0:T(1,128)} %bitcast.1, s32[1,16]{1,0:T(1,128)} %segments_hbm.1, bf16[2048,2048]{1,0:T(8,128)(2,1)} %wq_ref.1, bf16[2048,512]{1,0:T(8,128)(2,1)} %wkv_ref.1, bf16[2048,2048]{1,0:T(8,128)(2,1)} %wo_ref.1), custom_call_target="tpu_custom_call" | custom-call | flops 1207959552 | bytes 18874368 | tf_op jit(solution)/shard_map/pallas_call | solution.py:520
  33.5 1.5 %copy.8 = bf16[16,2048]{1,0:T(8,128)(2,1)} copy(bf16[16,2048]{1,0:T(8,128)(2,1)} %shard_map.64) | data formatting | bytes 131072

commit v5 on v4

--- a/solution.py
+++ b/solution.py
@@ -168,7 +168,7 @@
         weight_copies.append(
             pltpu.make_async_copy(wo_ref.at[piece, :], wo.at[piece, :], weight_sem.at[2 * CHUNKS + j])
         )
-    for copy in weight_copies[: 2 * CHUNKS]:
+    for copy in weight_copies[: 2]:
         copy.start()
 
     barrier = pltpu.get_barrier_semaphore()
@@ -223,7 +223,7 @@
         token_copy(c, 1, gx, (gx + 2) % side).start()
         token_copy(c, 0, gx, 1 + gx % 2).start()
         pl.when(middle)(token_copy(c, 2, gx, outer).start)
-    for copy in weight_copies[2 * CHUNKS :]:
+    for copy in weight_copies[2 :]:
         copy.start()
 
     def hand_on(c):

time: 35.1 us -> 35 us (level)
  no operation moved by 1% of the time
where the time goes in v5:
time: 35 us; the launch traced here: 34.8 us
  Pallas kernels  33.3 us (95%)
  local copies, waits for them, and re-layouts  1.47 us (4%)
    pallas_call x1, Pallas kernels, fused_on_device(): pl.pallas_call(fused_kernel, out_shape=jax.ShapeDtypeStruct((rows, w_out....  33.3 us
    unnamed x1, local copies, waits for them, and re-layouts  1.47 us

profile of v5, /device:TPU:0, one launch (start us, length us, event | category | flops | bytes accessed | tf_op | source)
XLA Modules:
  0.0 34.8 jit_solution(2532272979772309273)
XLA Ops:
  0.0 33.3 %shard_map.64 = bf16[16,2048]{1,0:T(8,128)(2,1)} custom-call(bf16[16,2048]{1,0:T(8,128)(2,1)} %tokens_ref.1, f32[1,2048]{1,0:T(1,128)} %bitcast.1, s32[1,16]{1,0:T(1,128)} %segments_hbm.1, bf16[2048,2048]{1,0:T(8,128)(2,1)} %wq_ref.1, bf16[2048,512]{1,0:T(8,128)(2,1)} %wkv_ref.1, bf16[2048,2048]{1,0:T(8,128)(2,1)} %wo_ref.1), custom_call_target="tpu_custom_call" | custom-call | flops 1207959552 | bytes 18874368 | tf_op jit(solution)/shard_map/pallas_call | solution.py:520
  33.3 1.5 %copy.8 = bf16[16,2048]{1,0:T(8,128)(2,1)} copy(bf16[16,2048]{1,0:T(8,128)(2,1)} %shard_map.64) | data formatting | bytes 131072
